TPU v7x, 32 devices: a whole 2x2x4 slice. The times are simulated.
32 devices in a mesh: dp: 4 (over y, x), ctx: 8 (over z, core).
Axes of the slice: x: 2, y: 2, z: 4, core: 2. Of those that a mesh axis runs over, the one named last changes fastest.
Arguments:
- query_heads: bfloat16 [8192, 16, 128], P(('dp', 'ctx')), parts along dimension 0, may hold values from -64 to 64
- key_heads: bfloat16 [8192, 8, 128], P(('dp', 'ctx')), parts along dimension 0, may hold values from -64 to 64
- value_heads: bfloat16 [8192, 8, 128], P(('dp', 'ctx')), parts along dimension 0, may hold values from -6 to 6
- grad_out: bfloat16 [8192, 16, 128], P(('dp', 'ctx')), parts along dimension 0, may hold values from -6 to 6
- doc_ids: int32 [8192], P('dp'), parts along dimension 0, may hold values from 0 to 2, as said below
Outputs:
- attended: bfloat16 [8192, 16, 128], P(('dp', 'ctx')), parts along dimension 0
- grad_query: bfloat16 [8192, 16, 128], P(('dp', 'ctx')), parts along dimension 0
- grad_key: bfloat16 [8192, 8, 128], P(('dp', 'ctx')), parts along dimension 0
- grad_value: bfloat16 [8192, 8, 128], P(('dp', 'ctx')), parts along dimension 0
There are 4 independent parts, one for each index of `dp`. A program takes and returns all parts, laid end to end along the dimension named above; each array names one. Nothing has to cross between parts.
Inputs may be any that keep to these rules, and one draw needn't show every extreme that they name: doc_ids starts at 0 and never falls; within each aligned block of 1024 tokens it rises by one exactly once, never at the block's first token.
All inputs are finite; a program needn't handle non-finite values.
Results may differ from a plain program's by a relative error of at most 0.012.
Values may be sent and summed in bfloat16 or wider, within the bound.
A program may use at most 64 MiB of HBM per device.

v0:
```python
import jax
import jax.numpy as jnp
from jax import lax
from jax.sharding import PartitionSpec as P

WINDOW = 1024


QUERY_SCALE = 168.0 ** (-0.5)


def from_behind(block, axis, distance):
    devices = range(lax.axis_size(axis))
    route = [(i - distance, i) for i in devices if i - distance in devices]
    return lax.ppermute(block, axis, route)


def group_grads(q_group, k_group, v_group, g_group, allowed):
    scores = QUERY_SCALE * jnp.einsum(
        "rad,cd->arc", q_group, k_group, preferred_element_type=jnp.float32
    )
    masked = jnp.where(allowed[None], scores, -jnp.inf)
    row_max = jnp.max(masked, axis=-1, keepdims=True)
    unnorm = jnp.exp(masked - row_max)
    weights = unnorm / jnp.sum(unnorm, axis=-1, keepdims=True)
    weights_b = weights.astype(jnp.bfloat16)
    attended = jnp.einsum(
        "arc,cd->rad", weights_b, v_group, preferred_element_type=jnp.float32
    ).astype(jnp.bfloat16)
    row_dot = jnp.sum(g_group.astype(jnp.float32) * attended.astype(jnp.float32), axis=-1)
    dprob = jnp.einsum("rad,cd->arc", g_group, v_group, preferred_element_type=jnp.float32)
    dscore = (weights * (dprob - jnp.transpose(row_dot)[..., None])).astype(jnp.bfloat16)
    grad_q = (
        QUERY_SCALE * jnp.einsum("arc,cd->rad", dscore, k_group, preferred_element_type=jnp.float32)
    ).astype(jnp.bfloat16)
    grad_k = (
        QUERY_SCALE * jnp.einsum("arc,rad->cd", dscore, q_group, preferred_element_type=jnp.float32)
    ).astype(jnp.bfloat16)
    grad_v = jnp.einsum(
        "arc,rad->cd", weights_b, g_group, preferred_element_type=jnp.float32
    ).astype(jnp.bfloat16)
    return (attended, grad_q, grad_k, grad_v)


def body(query_heads, key_heads, value_heads, grad_out, doc_ids):
    row_count = query_heads.shape[0]
    groups = key_heads.shape[1]
    head_size = key_heads.shape[2]
    reach = WINDOW // row_count
    piece_pos = lax.axis_index("ctx")
    earlier = []
    for offset in range(reach, 0, -1):
        earlier.append(from_behind((key_heads, value_heads), "ctx", offset))
    k_window = jnp.concatenate([pair[0] for pair in earlier] + [key_heads], 0)
    v_window = jnp.concatenate([pair[1] for pair in earlier] + [value_heads], 0)
    pad_docs = jnp.concatenate([jnp.full((WINDOW,), -1, jnp.int32), doc_ids], 0)
    first_row = piece_pos * row_count
    q_docs = lax.dynamic_slice_in_dim(doc_ids, first_row, row_count, 0)
    k_docs = lax.dynamic_slice_in_dim(pad_docs, first_row, WINDOW + row_count, 0)
    q_index = jnp.arange(row_count)[:, None]
    k_index = jnp.arange(WINDOW + row_count)[None, :]
    allowed = (
        (q_docs[:, None] == k_docs[None, :]) & (k_index > q_index) & (k_index <= q_index + WINDOW)
    )
    q_major = jnp.transpose(query_heads.reshape(row_count, groups, 2, head_size), (1, 0, 2, 3))
    g_major = jnp.transpose(grad_out.reshape(row_count, groups, 2, head_size), (1, 0, 2, 3))
    k_major = jnp.transpose(k_window, (1, 0, 2))
    v_major = jnp.transpose(v_window, (1, 0, 2))

    def per_group(operands):
        return group_grads(operands[0], operands[1], operands[2], operands[3], allowed)

    attended, grad_q, key_terms, value_terms = lax.map(
        per_group, (q_major, k_major, v_major, g_major)
    )
    attended = jnp.transpose(attended, (1, 0, 2, 3)).reshape(query_heads.shape)
    grad_q = jnp.transpose(grad_q, (1, 0, 2, 3)).reshape(query_heads.shape)
    key_terms = jnp.transpose(key_terms, (1, 0, 2))
    value_terms = jnp.transpose(value_terms, (1, 0, 2))
    key_terms, value_terms = lax.optimization_barrier((key_terms, value_terms))

    def term_for(offset):
        lower = (reach - offset) * row_count
        return (key_terms[lower : lower + row_count], value_terms[lower : lower + row_count])

    own_k, own_v = term_for(0)
    total_k = own_k.astype(jnp.float32)
    total_v = own_v.astype(jnp.float32)
    for offset in range(1, reach + 1):
        send_k, send_v = term_for(offset)
        back_k, back_v = from_behind((send_k, send_v), "ctx", -offset)
        total_k = total_k + back_k.astype(jnp.float32)
        total_v = total_v + back_v.astype(jnp.float32)
    return (attended, grad_q, total_k.astype(jnp.bfloat16), total_v.astype(jnp.bfloat16))


def solution(mesh):
    placed = (
        P(("dp", "ctx"), None, None),
        P(("dp", "ctx"), None, None),
        P(("dp", "ctx"), None, None),
        P(("dp", "ctx"), None, None),
        P("dp"),
    )
    return jax.shard_map(
        body,
        mesh=mesh,
        in_specs=placed,
        out_specs=(
            P(("dp", "ctx"), None, None),
            P(("dp", "ctx"), None, None),
            P(("dp", "ctx"), None, None),
            P(("dp", "ctx"), None, None),
        ),
        check_vma=False,
    )
```

profile of v0, /device:TPU:8, one launch (start us, length us, event | category | flops | bytes accessed | tf_op | source)
XLA Modules:
  0.0 362.6 jit_solution(2532376727952443927)
XLA Ops:
  2.1 5.3 %collective-permute-start = (bf16[256,8,128]{0,2,1:T(8,128)(2,1)S(1)}, bf16[256,8,128]{0,2,1:T(8,128)(2,1)}, u32[]{:S(2)}, u32[]{:S(2)}) collective-permute-start(bf16[256,8,128]{0,2,1:T(8,128)(2,1)S(1)} %copy.15), channel_id=1, source_target_pairs={{0,4},{1,5},{2,6},{3,7},{8,12},{9,13},{10,14},{11,15},{16,20},{17,... | collective-permute-start | bytes 1572872 | tf_op jit(solution)/shard_map/ppermute | solution.py:15
  20.2 14.5 %collective-permute-done = bf16[256,8,128]{0,2,1:T(8,128)(2,1)} collective-permute-done((bf16[256,8,128]{0,2,1:T(8,128)(2,1)S(1)}, bf16[256,8,128]{0,2,1:T(8,128)(2,1)}, u32[]{:S(2)}, u32[]{:S(2)}) %collective-permute-start) | collective-permute-done | bytes 524320 | tf_op jit(solution)/shard_map/ppermute | solution.py:15
  34.7 5.5 %collective-permute-start.4 = (bf16[256,8,128]{2,0,1:T(8,128)(2,1)}, bf16[256,8,128]{2,0,1:T(8,128)(2,1)S(1)}, u32[]{:S(2)}, u32[]{:S(2)}) collective-permute-start(bf16[256,8,128]{2,0,1:T(8,128)(2,1)} %copy.20), channel_id=1, source_target_pairs={{0,4},{1,5},{2,6},{3,7},{8,12},{9,13},{10,14},{11,15},{16,20},{17,... | collective-permute-start | bytes 1572872 | tf_op jit(solution)/shard_map/ppermute | solution.py:15
  41.2 8.9 %collective-permute-done.1 = bf16[256,8,128]{0,2,1:T(8,128)(2,1)} collective-permute-done((bf16[256,8,128]{0,2,1:T(8,128)(2,1)S(1)}, bf16[256,8,128]{0,2,1:T(8,128)(2,1)}, u32[]{:S(2)}, u32[]{:S(2)}) %collective-permute-start.1) | collective-permute-done | bytes 524320 | tf_op jit(solution)/shard_map/ppermute | solution.py:15
  50.1 4.5 %collective-permute-start.5 = (bf16[256,8,128]{2,0,1:T(8,128)(2,1)}, bf16[256,8,128]{2,0,1:T(8,128)(2,1)S(1)}, u32[]{:S(2)}, u32[]{:S(2)}) collective-permute-start(bf16[256,8,128]{2,0,1:T(8,128)(2,1)} %copy.20), channel_id=1, source_target_pairs={{0,3},{1,4},{2,5},{3,6},{4,7},{8,11},{9,12},{10,13},{11,14},{12,15... | collective-permute-start | bytes 1572872 | tf_op jit(solution)/shard_map/ppermute | solution.py:15
  55.7 9.4 %collective-permute-done.2 = bf16[256,8,128]{0,2,1:T(8,128)(2,1)} collective-permute-done((bf16[256,8,128]{0,2,1:T(8,128)(2,1)S(1)}, bf16[256,8,128]{0,2,1:T(8,128)(2,1)}, u32[]{:S(2)}, u32[]{:S(2)}) %collective-permute-start.2) | collective-permute-done | bytes 524320 | tf_op jit(solution)/shard_map/ppermute | solution.py:15
  65.1 4.7 %collective-permute-start.6 = (bf16[256,8,128]{2,0,1:T(8,128)(2,1)}, bf16[256,8,128]{2,0,1:T(8,128)(2,1)S(1)}, u32[]{:S(2)}, u32[]{:S(2)}) collective-permute-start(bf16[256,8,128]{2,0,1:T(8,128)(2,1)} %copy.20), channel_id=1, source_target_pairs={{0,2},{1,3},{2,4},{3,5},{4,6},{5,7},{8,10},{9,11},{10,12},{11,13},... | collective-permute-start | bytes 1572872 | tf_op jit(solution)/shard_map/ppermute | solution.py:15
  72.1 13.3 %collective-permute-done.4 = bf16[256,8,128]{2,0,1:T(8,128)(2,1)S(1)} collective-permute-done((bf16[256,8,128]{2,0,1:T(8,128)(2,1)}, bf16[256,8,128]{2,0,1:T(8,128)(2,1)S(1)}, u32[]{:S(2)}, u32[]{:S(2)}) %collective-permute-start.4) | collective-permute-done | bytes 524320 | tf_op jit(solution)/shard_map/ppermute | solution.py:15
  85.4 11.2 %collective-permute-done.5 = bf16[256,8,128]{2,0,1:T(8,128)(2,1)S(1)} collective-permute-done((bf16[256,8,128]{2,0,1:T(8,128)(2,1)}, bf16[256,8,128]{2,0,1:T(8,128)(2,1)S(1)}, u32[]{:S(2)}, u32[]{:S(2)}) %collective-permute-start.5) | collective-permute-done | bytes 524320 | tf_op jit(solution)/shard_map/ppermute | solution.py:15
  96.7 11.2 %collective-permute-done.6 = bf16[256,8,128]{2,0,1:T(8,128)(2,1)S(1)} collective-permute-done((bf16[256,8,128]{2,0,1:T(8,128)(2,1)}, bf16[256,8,128]{2,0,1:T(8,128)(2,1)S(1)}, u32[]{:S(2)}, u32[]{:S(2)}) %collective-permute-start.6) | collective-permute-done | bytes 524320 | tf_op jit(solution)/shard_map/ppermute | solution.py:15
  109.7 107.3 %while.17 = (s32[]{:T(128)}, bf16[8,256,2,128]{1,3,2,0:T(8,128)(2,1)}, bf16[8,256,2,128]{1,3,2,0:T(8,128)(2,1)}, bf16[8,1280,128]{2,1,0:T(8,128)(2,1)}, bf16[8,1...) while((s32[]{:T(128)}, ...), condition=%wide.region_4.5_spmd.clone, body=%wide.region_0.4_spmd.clone.sunk | while | flops 1015776000 | bytes 19553416 | solution.py:73
  120.9 2.2 fusion.106
  134.4 2.2 fusion.106
  216.9 13.2 %copy_bitcast_fusion = (bf16[1280,8,128]{2,1,0:T(8,128)(2,1)S(1)}, bf16[1280,8,128]{2,1,0:T(8,128)(2,1)S(1)}) fusion(bf16[8,1280,128]{2,1,0:T(8,128)(2,1)} %get-tuple-element.64, bf16[8,1280,128]{2,1,0:T(8,128)(2,1)} %get-tuple-element.63), kind=kLoop, calls=%fused_computation.61 | loop fusion | bytes 10485760 | tf_op jit(solution)/shard_map/transpose | solution.py:79
  241.0 4.8 %collective-permute-done.8 = bf16[256,8,128]{2,1,0:T(8,128)(2,1)S(1)} collective-permute-done((bf16[256,8,128]{2,1,0:T(8,128)(2,1)S(1)}, bf16[256,8,128]{2,1,0:T(8,128)(2,1)S(1)}, u32[]{:S(2)}, u32[]{:S(2)}) %collective-permute-start.8) | collective-permute-done | bytes 524320 | tf_op jit(solution)/shard_map/ppermute | solution.py:15
  247.1 23.9 %collective-permute-done.11 = bf16[256,8,128]{2,1,0:T(8,128)(2,1)} collective-permute-done((bf16[256,8,128]{2,1,0:T(8,128)(2,1)S(1)}, bf16[256,8,128]{2,1,0:T(8,128)(2,1)}, u32[]{:S(2)}, u32[]{:S(2)}) %collective-permute-start.11) | collective-permute-done | bytes 524320 | tf_op jit(solution)/shard_map/ppermute | solution.py:15
  272.3 20.3 %collective-permute-done.10 = bf16[256,8,128]{2,1,0:T(8,128)(2,1)} collective-permute-done((bf16[256,8,128]{2,1,0:T(8,128)(2,1)S(1)}, bf16[256,8,128]{2,1,0:T(8,128)(2,1)}, u32[]{:S(2)}, u32[]{:S(2)}) %collective-permute-start.10) | collective-permute-done | bytes 524320 | tf_op jit(solution)/shard_map/ppermute | solution.py:15
  294.5 3.7 %copy.27 = bf16[256,8,2,128]{3,2,1,0:T(2,128)(2,1)} copy(bf16[256,8,2,128]{0,3,2,1:T(8,128)(2,1)} %bitcast.169) | data formatting | bytes 2097152 | tf_op jit(solution)/shard_map/transpose | solution.py:76
  298.2 3.7 %copy.28 = bf16[256,8,2,128]{3,2,1,0:T(2,128)(2,1)} copy(bf16[256,8,2,128]{0,3,2,1:T(8,128)(2,1)} %bitcast.168) | data formatting | bytes 2097152 | tf_op jit(solution)/shard_map/transpose | solution.py:77
  301.8 23.3 %collective-permute-done.9 = bf16[256,8,128]{2,1,0:T(8,128)(2,1)} collective-permute-done((bf16[256,8,128]{2,1,0:T(8,128)(2,1)}, bf16[256,8,128]{2,1,0:T(8,128)(2,1)}, u32[]{:S(2)}, u32[]{:S(2)}) %collective-permute-start.9) | collective-permute-done | bytes 524320 | tf_op jit(solution)/shard_map/ppermute | solution.py:15
  325.2 2.6 add_convert_fusion.1
  327.8 10.8 %collective-permute-done.14 = bf16[256,8,128]{2,1,0:T(8,128)(2,1)} collective-permute-done((bf16[256,8,128]{2,1,0:T(8,128)(2,1)}, bf16[256,8,128]{2,1,0:T(8,128)(2,1)}, u32[]{:S(2)}, u32[]{:S(2)}) %collective-permute-start.14) | collective-permute-done | bytes 524320 | tf_op jit(solution)/shard_map/ppermute | solution.py:15
  338.6 21.4 %collective-permute-done.13 = bf16[256,8,128]{2,1,0:T(8,128)(2,1)} collective-permute-done((bf16[256,8,128]{2,1,0:T(8,128)(2,1)}, bf16[256,8,128]{2,1,0:T(8,128)(2,1)}, u32[]{:S(2)}, u32[]{:S(2)}) %collective-permute-start.13) | collective-permute-done | bytes 524320 | tf_op jit(solution)/shard_map/ppermute | solution.py:15
  360.0 2.6 add_convert_fusion
  (123 shorter events, 138.4 us)
Async XLA Ops:
  0.6 16.6 %copy-start.4 = (bf16[256,16,128]{2,1,0:T(8,128)(2,1)S(1)}, bf16[256,16,128]{2,1,0:T(8,128)(2,1)}, u32[]{:S(2)}) copy-start(bf16[256,16,128]{2,1,0:T(8,128)(2,1)} %param.7) | copy-start | bytes 3145732
  0.6 17.9 %copy-start.5 = (bf16[256,16,128]{2,1,0:T(8,128)(2,1)S(1)}, bf16[256,16,128]{2,1,0:T(8,128)(2,1)}, u32[]{:S(2)}) copy-start(bf16[256,16,128]{2,1,0:T(8,128)(2,1)} %param.10) | copy-start | bytes 3145732
  2.1 17.9 %copy-start.6 = (s32[2048]{0:T(1024)S(1)}, s32[2048]{0:T(1024)}, u32[]{:S(2)}) copy-start(s32[2048]{0:T(1024)} %param.11) | copy-start | bytes 24580
  2.1 32.5 %collective-permute-start = (bf16[256,8,128]{0,2,1:T(8,128)(2,1)S(1)}, bf16[256,8,128]{0,2,1:T(8,128)(2,1)}, u32[]{:S(2)}, u32[]{:S(2)}) collective-permute-start(bf16[256,8,128]{0,2,1:T(8,128)(2,1)S(1)} %copy.15), channel_id=1, source_target_pairs={{0,4},{1,5},{2,6},{3,7},{8,12},{9,13},{10,14},{11,15},{16,20},{17,... | collective-permute-start | bytes 1572872 | tf_op jit(solution)/shard_map/ppermute | solution.py:15
  7.4 42.7 %collective-permute-start.1 = (bf16[256,8,128]{0,2,1:T(8,128)(2,1)S(1)}, bf16[256,8,128]{0,2,1:T(8,128)(2,1)}, u32[]{:S(2)}, u32[]{:S(2)}) collective-permute-start(bf16[256,8,128]{0,2,1:T(8,128)(2,1)S(1)} %copy.15), channel_id=1, source_target_pairs={{0,3},{1,4},{2,5},{3,6},{4,7},{8,11},{9,12},{10,13},{11,14},{12,15... | collective-permute-start | bytes 1572872 | tf_op jit(solution)/shard_map/ppermute | solution.py:15
  9.5 55.6 %collective-permute-start.2 = (bf16[256,8,128]{0,2,1:T(8,128)(2,1)S(1)}, bf16[256,8,128]{0,2,1:T(8,128)(2,1)}, u32[]{:S(2)}, u32[]{:S(2)}) collective-permute-start(bf16[256,8,128]{0,2,1:T(8,128)(2,1)S(1)} %copy.15), channel_id=1, source_target_pairs={{0,2},{1,3},{2,4},{3,5},{4,6},{5,7},{8,10},{9,11},{10,12},{11,13},... | collective-permute-start | bytes 1572872 | tf_op jit(solution)/shard_map/ppermute | solution.py:15
  11.4 59.5 %collective-permute-start.3 = (bf16[256,8,128]{0,2,1:T(8,128)(2,1)S(1)}, bf16[256,8,128]{0,2,1:T(8,128)(2,1)}, u32[]{:S(2)}, u32[]{:S(2)}) collective-permute-start(bf16[256,8,128]{0,2,1:T(8,128)(2,1)S(1)} %copy.15), channel_id=1, source_target_pairs={{0,1},{1,2},{2,3},{3,4},{4,5},{5,6},{6,7},{8,9},{9,10},{10,11},{11... | collective-permute-start | bytes 1572872 | tf_op jit(solution)/shard_map/ppermute | solution.py:15
  15.3 92.6 %collective-permute-start.7 = (bf16[256,8,128]{2,0,1:T(8,128)(2,1)}, bf16[256,8,128]{2,0,1:T(8,128)(2,1)S(1)}, u32[]{:S(2)}, u32[]{:S(2)}) collective-permute-start(bf16[256,8,128]{2,0,1:T(8,128)(2,1)} %copy.20), channel_id=1, source_target_pairs={{0,1},{1,2},{2,3},{3,4},{4,5},{5,6},{6,7},{8,9},{9,10},{10,11},{11... | collective-permute-start | bytes 1572872 | tf_op jit(solution)/shard_map/ppermute | solution.py:15
  34.7 50.7 %collective-permute-start.4 = (bf16[256,8,128]{2,0,1:T(8,128)(2,1)}, bf16[256,8,128]{2,0,1:T(8,128)(2,1)S(1)}, u32[]{:S(2)}, u32[]{:S(2)}) collective-permute-start(bf16[256,8,128]{2,0,1:T(8,128)(2,1)} %copy.20), channel_id=1, source_target_pairs={{0,4},{1,5},{2,6},{3,7},{8,12},{9,13},{10,14},{11,15},{16,20},{17,... | collective-permute-start | bytes 1572872 | tf_op jit(solution)/shard_map/ppermute | solution.py:15
  50.1 46.4 %collective-permute-start.5 = (bf16[256,8,128]{2,0,1:T(8,128)(2,1)}, bf16[256,8,128]{2,0,1:T(8,128)(2,1)S(1)}, u32[]{:S(2)}, u32[]{:S(2)}) collective-permute-start(bf16[256,8,128]{2,0,1:T(8,128)(2,1)} %copy.20), channel_id=1, source_target_pairs={{0,3},{1,4},{2,5},{3,6},{4,7},{8,11},{9,12},{10,13},{11,14},{12,15... | collective-permute-start | bytes 1572872 | tf_op jit(solution)/shard_map/ppermute | solution.py:15
  65.1 42.7 %collective-permute-start.6 = (bf16[256,8,128]{2,0,1:T(8,128)(2,1)}, bf16[256,8,128]{2,0,1:T(8,128)(2,1)S(1)}, u32[]{:S(2)}, u32[]{:S(2)}) collective-permute-start(bf16[256,8,128]{2,0,1:T(8,128)(2,1)} %copy.20), channel_id=1, source_target_pairs={{0,2},{1,3},{2,4},{3,5},{4,6},{5,7},{8,10},{9,11},{10,12},{11,13},... | collective-permute-start | bytes 1572872 | tf_op jit(solution)/shard_map/ppermute | solution.py:15
  72.0 36.0 %copy-start.1 = (bf16[256,8,128]{2,1,0:T(8,128)(2,1)S(1)}, bf16[256,8,128]{2,1,0:T(8,128)(2,1)}, u32[]{:S(2)}) copy-start(bf16[256,8,128]{2,1,0:T(8,128)(2,1)} %param.8) | copy-start | bytes 1572868
  72.1 36.0 %copy-start.2 = (bf16[1280,8,128]{0,2,1:T(8,128)(2,1)}, bf16[1280,8,128]{0,2,1:T(8,128)(2,1)S(1)}, u32[]{:S(2)}) copy-start(bf16[1280,8,128]{0,2,1:T(8,128)(2,1)S(1)} %constant_dynamic-update-slice_fusion) | copy-start | bytes 7864324
  108.1 1.5 copy-start.3
  230.2 8.9 %copy-start = (bf16[1280,8,128]{2,1,0:T(8,128)(2,1)}, bf16[1280,8,128]{2,1,0:T(8,128)(2,1)S(1)}, u32[]{:S(2)}) copy-start(bf16[1280,8,128]{2,1,0:T(8,128)(2,1)S(1)} %get-tuple-element.65) | copy-start | bytes 7864324
  231.3 14.5 %collective-permute-start.8 = (bf16[256,8,128]{2,1,0:T(8,128)(2,1)S(1)}, bf16[256,8,128]{2,1,0:T(8,128)(2,1)S(1)}, u32[]{:S(2)}, u32[]{:S(2)}) collective-permute-start(bf16[256,8,128]{2,1,0:T(8,128)(2,1)S(1)} %get-tuple-element.128), channel_id=1, source_target_pairs={{1,0},{2,1},{3,2},{4,3},{5,4},{6,5},{7,6},{9,8},{10,9},{11,10},{12... | collective-permute-start | bytes 1572872 | tf_op jit(solution)/shard_map/ppermute | solution.py:15
  233.2 37.8 %collective-permute-start.11 = (bf16[256,8,128]{2,1,0:T(8,128)(2,1)S(1)}, bf16[256,8,128]{2,1,0:T(8,128)(2,1)}, u32[]{:S(2)}, u32[]{:S(2)}) collective-permute-start(bf16[256,8,128]{2,1,0:T(8,128)(2,1)S(1)} %get-tuple-element.129), channel_id=1, source_target_pairs={{4,0},{5,1},{6,2},{7,3},{12,8},{13,9},{14,10},{15,11},{20,16},{21,... | collective-permute-start | bytes 1572872 | tf_op jit(solution)/shard_map/ppermute | solution.py:15
  234.5 58.1 %collective-permute-start.10 = (bf16[256,8,128]{2,1,0:T(8,128)(2,1)S(1)}, bf16[256,8,128]{2,1,0:T(8,128)(2,1)}, u32[]{:S(2)}, u32[]{:S(2)}) collective-permute-start(bf16[256,8,128]{2,1,0:T(8,128)(2,1)S(1)} %get-tuple-element.130), channel_id=1, source_target_pairs={{3,0},{4,1},{5,2},{6,3},{7,4},{11,8},{12,9},{13,10},{14,11},{15,12... | collective-permute-start | bytes 1572872 | tf_op jit(solution)/shard_map/ppermute | solution.py:15
  235.8 89.4 %collective-permute-start.9 = (bf16[256,8,128]{2,1,0:T(8,128)(2,1)}, bf16[256,8,128]{2,1,0:T(8,128)(2,1)}, u32[]{:S(2)}, u32[]{:S(2)}) collective-permute-start(bf16[256,8,128]{2,1,0:T(8,128)(2,1)} %get-tuple-element.131), channel_id=1, source_target_pairs={{2,0},{3,1},{4,2},{5,3},{6,4},{7,5},{10,8},{11,9},{12,10},{13,11},... | collective-permute-start | bytes 1572872 | tf_op jit(solution)/shard_map/ppermute | solution.py:15
  239.1 88.8 %collective-permute-start.12 = (bf16[256,8,128]{2,1,0:T(8,128)(2,1)}, bf16[256,8,128]{2,1,0:T(8,128)(2,1)}, u32[]{:S(2)}, u32[]{:S(2)}) collective-permute-start(bf16[256,8,128]{2,1,0:T(8,128)(2,1)} %get-tuple-element.124), channel_id=1, source_target_pairs={{1,0},{2,1},{3,2},{4,3},{5,4},{6,5},{7,6},{9,8},{10,9},{11,10},{12... | collective-permute-start | bytes 1572872 | tf_op jit(solution)/shard_map/ppermute | solution.py:15
  245.8 82.1 %collective-permute-start.15 = (bf16[256,8,128]{2,1,0:T(8,128)(2,1)}, bf16[256,8,128]{2,1,0:T(8,128)(2,1)}, u32[]{:S(2)}, u32[]{:S(2)}) collective-permute-start(bf16[256,8,128]{2,1,0:T(8,128)(2,1)} %get-tuple-element.125), channel_id=1, source_target_pairs={{4,0},{5,1},{6,2},{7,3},{12,8},{13,9},{14,10},{15,11},{20,16},{21,... | collective-permute-start | bytes 1572872 | tf_op jit(solution)/shard_map/ppermute | solution.py:15
  271.0 67.6 %collective-permute-start.14 = (bf16[256,8,128]{2,1,0:T(8,128)(2,1)}, bf16[256,8,128]{2,1,0:T(8,128)(2,1)}, u32[]{:S(2)}, u32[]{:S(2)}) collective-permute-start(bf16[256,8,128]{2,1,0:T(8,128)(2,1)} %get-tuple-element.126), channel_id=1, source_target_pairs={{3,0},{4,1},{5,2},{6,3},{7,4},{11,8},{12,9},{13,10},{14,11},{15,12... | collective-permute-start | bytes 1572872 | tf_op jit(solution)/shard_map/ppermute | solution.py:15
  292.6 67.4 %collective-permute-start.13 = (bf16[256,8,128]{2,1,0:T(8,128)(2,1)}, bf16[256,8,128]{2,1,0:T(8,128)(2,1)}, u32[]{:S(2)}, u32[]{:S(2)}) collective-permute-start(bf16[256,8,128]{2,1,0:T(8,128)(2,1)} %get-tuple-element.127), channel_id=1, source_target_pairs={{2,0},{3,1},{4,2},{5,3},{6,4},{7,5},{10,8},{11,9},{12,10},{13,11},... | collective-permute-start | bytes 1572872 | tf_op jit(solution)/shard_map/ppermute | solution.py:15
where the time goes:
time: 365 us; the launch traced here: 363 us
  waiting for transfers between devices  173 us (47%)
  matrix products  94.7 us (26%)
  starting transfers between devices  40.6 us (11%)
  local copies, waits for them, and re-layouts  35.6 us (10%)
  other arithmetic  17.7 us (5%)
    ppermute x16, waiting for transfers between devices, from_behind(): return lax.ppermute(block, axis, route)  173 us
    ppermute x16, starting transfers between devices, from_behind(): return lax.ppermute(block, axis, route)  40.6 us
    dot_general x8, matrix products, group_grads(): jnp.einsum('arc,rad->cd', weights_b, g_group, preferred_element_type=jnp....  17.2 us
    dot_general x8, matrix products, group_grads(): jnp.einsum('arc,rad->cd', dscore, q_group, preferred_element_type=jnp.flo...  17.1 us
    dot_general x8, matrix products, group_grads(): jnp.einsum('arc,cd->rad', dscore, k_group, preferred_element_type=jnp.flo...  16.1 us
    sub x8, matrix products, group_grads(): unnorm = jnp.exp(masked - row_max)  16.1 us
    dot_general x8, matrix products, group_grads(): jnp.einsum('arc,cd->rad', weights_b, v_group, preferred_element_type=jnp....  15.8 us
    transpose x1, local copies, waits for them, and re-layouts, body(): value_terms = jnp.transpose(value_terms, (1, 0, 2))  13.2 us
  transfers between devices with their start and end apart: 16, of which 12 were waited for; matrix products, arithmetic and copies ran while one was open for 6% of the time, Pallas kernels for 0%

commit v1 on v0

v1 whole, which is shorter than its diff:
```python
import functools

import jax
import jax.numpy as jnp
from jax import lax
from jax.experimental import pallas as pl
from jax.experimental.pallas import tpu as pltpu
from jax.sharding import PartitionSpec as P

WINDOW = 1024
QUERY_SCALE = 168.0 ** (-0.5)
F32 = jnp.float32
BF16 = jnp.bfloat16
MASKED = -1e30


def remote(src, dst, send_sem, recv_sem, ctx):
    return pltpu.make_async_remote_copy(
        src_ref=src,
        dst_ref=dst,
        send_sem=send_sem,
        recv_sem=recv_sem,
        device_id={"ctx": ctx},
        device_id_type=pl.DeviceIdType.MESH,
    )


def kernel(
    chips, half,
    q_ref, g_ref, k_ref, v_ref, qd_ref, kd_ref,
    o_ref, dq_ref, dk_ref, dv_ref,
    qs, gs, kw, vw, bias, acc, own_s, far_s, far_r, mid_s, mid_r, o_s, dq_s, fin_s,
    swap_send, swap_recv, near_send, near_recv, fwd_send, fwd_recv,
    far_send, far_recv, mid_send, mid_recv, out_send, out_recv, fin_send, fin_recv,
):
    rows = k_ref.shape[1]
    me = lax.axis_index("ctx")
    z = lax.div(me, 2)
    c = lax.rem(me, 2)
    partner = z * 2 + (1 - c)
    has_prev = z > 0
    has_prev2 = z > 1
    has_next = z < chips - 1
    mine = c * half

    barrier = pltpu.get_barrier_semaphore()

    def greet(ctx):
        pl.semaphore_signal(
            barrier, inc=1, device_id={"ctx": ctx}, device_id_type=pl.DeviceIdType.MESH
        )

    greet(partner)

    @pl.when(has_prev)
    def _():
        greet(z * 2 - 2)
        greet(z * 2 - 1)

    @pl.when(has_next)
    def _():
        greet(z * 2 + 2)
        greet(z * 2 + 3)

    links = jnp.where(has_prev, 1, 0) + jnp.where(has_next, 1, 0)
    pl.semaphore_wait(barrier, 1 + 2 * links)

    def swap_copies(hl):
        theirs = (1 - c) * half + hl
        return [
            remote(k_ref.at[theirs], kw.at[hl, 4 + c], swap_send.at[hl, 0], swap_recv.at[hl, 0], partner),
            remote(v_ref.at[theirs], vw.at[hl, 4 + c], swap_send.at[hl, 1], swap_recv.at[hl, 1], partner),
            remote(q_ref.at[theirs], qs.at[hl, c], swap_send.at[hl, 2], swap_recv.at[hl, 2], partner),
            remote(g_ref.at[theirs], gs.at[hl, c], swap_send.at[hl, 3], swap_recv.at[hl, 3], partner),
        ]

    def near_copies(hl, to):
        head = to * half + hl
        return [
            remote(k_ref.at[head], kw.at[hl, 2 + c], near_send.at[to, hl, 0], near_recv.at[c, hl, 0], z * 2 + 2 + to),
            remote(v_ref.at[head], vw.at[hl, 2 + c], near_send.at[to, hl, 1], near_recv.at[c, hl, 1], z * 2 + 2 + to),
        ]

    def near_arrivals(hl, sender):
        return [
            remote(k_ref.at[hl], kw.at[hl, 2 + sender], near_send.at[0, hl, 0], near_recv.at[sender, hl, 0], partner),
            remote(v_ref.at[hl], vw.at[hl, 2 + sender], near_send.at[0, hl, 1], near_recv.at[sender, hl, 1], partner),
        ]

    def fwd_copies(hl):
        return [
            remote(kw.at[hl, pl.ds(2, 2)], kw.at[hl, pl.ds(0, 2)], fwd_send.at[hl, 0], fwd_recv.at[hl, 0], me + 2),
            remote(vw.at[hl, pl.ds(2, 2)], vw.at[hl, pl.ds(0, 2)], fwd_send.at[hl, 1], fwd_recv.at[hl, 1], me + 2),
        ]

    def far_copy(hl):
        return remote(far_s.at[hl], far_r.at[hl], far_send.at[hl], far_recv.at[hl], me - 2)

    def mid_copy(hl):
        return remote(mid_s.at[hl], mid_r.at[hl], mid_send.at[hl], mid_recv.at[hl], me - 2)

    def out_copies(hl):
        return [
            remote(o_s.at[hl, 1 - c], o_ref.at[mine + hl], out_send.at[hl, 0], out_recv.at[hl, 0], partner),
            remote(dq_s.at[hl, 1 - c], dq_ref.at[mine + hl], out_send.at[hl, 1], out_recv.at[hl, 1], partner),
        ]

    def fin_copies(hl):
        return [
            remote(fin_s.at[hl, 0], dk_ref.at[mine + hl], fin_send.at[hl, 0], fin_recv.at[hl, 0], partner),
            remote(fin_s.at[hl, 1], dv_ref.at[mine + hl], fin_send.at[hl, 1], fin_recv.at[hl, 1], partner),
        ]

    def heads(body):
        def step(hl, carry):
            body(hl)
            return carry

        lax.fori_loop(0, half, step, 0)

    def begin(hl):
        @pl.when(has_next)
        def _():
            for to in range(2):
                for copy in near_copies(hl, to):
                    copy.start()

        for copy in swap_copies(hl):
            copy.start()

    heads(begin)

    def local(hl):
        kw[hl, 4 + c] = k_ref[mine + hl]
        vw[hl, 4 + c] = v_ref[mine + hl]
        qs[hl, c] = q_ref[mine + hl]
        gs[hl, c] = g_ref[mine + hl]

        @pl.when(z == 0)
        def _():
            kw[hl, 2:4] = jnp.zeros((2,) + kw.shape[2:], BF16)
            vw[hl, 2:4] = jnp.zeros((2,) + kw.shape[2:], BF16)

        @pl.when(z < 2)
        def _():
            kw[hl, 0:2] = jnp.zeros((2,) + kw.shape[2:], BF16)
            vw[hl, 0:2] = jnp.zeros((2,) + kw.shape[2:], BF16)

    heads(local)

    width = WINDOW + rows
    for piece in range(2):
        lower = piece * rows
        q_index = lax.broadcasted_iota(jnp.int32, (rows, width), 0)
        k_index = lax.broadcasted_iota(jnp.int32, (rows, width), 1)
        same = qd_ref[lower : lower + rows, :] == kd_ref[:, lower : lower + width]
        allowed = same & (k_index > q_index) & (k_index <= q_index + WINDOW)
        bias[piece] = jnp.where(allowed, 0.0, MASKED).astype(F32)

    blocks = width // rows

    def attend(hl, piece):
        q2 = qs[hl, piece].reshape(2 * rows, -1)
        g2 = gs[hl, piece].reshape(2 * rows, -1)
        kk = kw[hl, pl.ds(piece, blocks)].reshape(width, -1)
        vv = vw[hl, pl.ds(piece, blocks)].reshape(width, -1)
        across = (((1,), (1,)), ((), ()))
        along = (((1,), (0,)), ((), ()))
        down = (((0,), (0,)), ((), ()))
        s = lax.dot_general(q2, kk, across, preferred_element_type=F32)
        s = s.reshape(2, rows, width) + bias[piece][None]
        top = jnp.max(s, axis=-1, keepdims=True)
        p = jnp.exp((s - top) * QUERY_SCALE)
        w = (p * (1.0 / jnp.sum(p, axis=-1, keepdims=True))).reshape(2 * rows, width)
        wb = w.astype(BF16)
        o = lax.dot_general(wb, vv, along, preferred_element_type=F32).astype(BF16)
        o_s[hl, piece] = o.reshape(2, rows, -1)
        row_dot = jnp.sum(g2.astype(F32) * o.astype(F32), axis=-1, keepdims=True)
        dp = lax.dot_general(g2, vv, across, preferred_element_type=F32)
        ds = (w * (dp - row_dot)).astype(BF16)
        dq = QUERY_SCALE * lax.dot_general(ds, kk, along, preferred_element_type=F32)
        dq_s[hl, piece] = dq.astype(BF16).reshape(2, rows, -1)
        dk = QUERY_SCALE * lax.dot_general(ds, q2, down, preferred_element_type=F32)
        dv = lax.dot_general(wb, g2, down, preferred_element_type=F32)
        acc[0, pl.ds(piece, blocks)] += dk.reshape(blocks, rows, -1)
        acc[1, pl.ds(piece, blocks)] += dv.reshape(blocks, rows, -1)

    def pass_mid(hl):
        @pl.when(has_prev & has_next)
        def _():
            far_copy(hl).wait_recv()
            mid_s[hl] = (mid_s[hl].astype(F32) + far_r[hl].astype(F32)).astype(BF16)

        @pl.when(has_prev)
        def _():
            mid_copy(hl).start()

    def stage(hl):
        @pl.when(has_prev)
        def _():
            for sender in range(2):
                for copy in near_arrivals(hl, sender):
                    copy.wait_recv()

        @pl.when(has_prev & has_next)
        def _():
            for copy in fwd_copies(hl):
                copy.start()

        for copy in swap_copies(hl):
            copy.wait_recv()

        @pl.when(has_prev2)
        def _():
            for copy in fwd_copies(hl):
                copy.wait_recv()

        acc[...] = jnp.zeros_like(acc)

        def per_piece(piece, carry):
            attend(hl, piece)
            return carry

        lax.fori_loop(0, 2, per_piece, 0)
        own_s[hl] = acc[:, 4:6]
        mid_s[hl] = acc[:, 2:4].astype(BF16)
        far_s[hl] = acc[:, 0:2].astype(BF16)

        @pl.when(has_prev2)
        def _():
            far_copy(hl).start()

        for copy in out_copies(hl):
            copy.start()
        o_ref[mine + hl] = o_s[hl, c]
        dq_ref[mine + hl] = dq_s[hl, c]

        @pl.when(hl > 0)
        def _():
            pass_mid(hl - 1)

    heads(stage)
    pass_mid(half - 1)

    def finish(hl):
        @pl.when(has_next)
        def _():
            mid_copy(hl).wait_recv()
            own_s[hl] = own_s[hl] + mid_r[hl].astype(F32)

        fin_s[hl] = own_s[hl, :, 1 - c].astype(BF16)
        for copy in fin_copies(hl):
            copy.start()
        dk_ref[mine + hl] = own_s[hl, 0, c].astype(BF16)
        dv_ref[mine + hl] = own_s[hl, 1, c].astype(BF16)

    heads(finish)

    def drain(hl):
        @pl.when(has_next)
        def _():
            for to in range(2):
                for copy in near_copies(hl, to):
                    copy.wait_send()

        @pl.when(has_prev & has_next)
        def _():
            for copy in fwd_copies(hl):
                copy.wait_send()

        for copy in swap_copies(hl):
            copy.wait_send()

        @pl.when(has_prev2)
        def _():
            far_copy(hl).wait_send()

        @pl.when(has_prev)
        def _():
            mid_copy(hl).wait_send()

        for copy in out_copies(hl) + fin_copies(hl):
            copy.wait()

    heads(drain)


def body(query_heads, key_heads, value_heads, grad_out, doc_ids):
    rows, groups, size = key_heads.shape
    half = groups // 2
    count = lax.axis_size("ctx")
    chip = lax.div(lax.axis_index("ctx"), 2)
    first_row = chip * (2 * rows)
    pad_docs = jnp.concatenate([jnp.full((WINDOW,), -1, jnp.int32), doc_ids], 0)
    q_docs = lax.dynamic_slice_in_dim(doc_ids, first_row, 2 * rows, 0)[:, None]
    k_docs = lax.dynamic_slice_in_dim(pad_docs, first_row, WINDOW + 2 * rows, 0)[None, :]

    def paired(x):
        return jnp.transpose(x.reshape(rows, groups, 2, size), (1, 2, 0, 3))

    def unpaired(x):
        return jnp.transpose(x, (2, 0, 1, 3)).reshape(query_heads.shape)

    wide = jax.ShapeDtypeStruct((groups, 2, rows, size), BF16)
    slim = jax.ShapeDtypeStruct((groups, rows, size), BF16)
    slots = (WINDOW + 2 * rows) // rows
    vmem = pl.BlockSpec(memory_space=pltpu.VMEM)
    dma = pltpu.SemaphoreType.DMA
    part = (half, 2, 2, rows, size)
    attended, grad_q, grad_k, grad_v = pl.pallas_call(
        functools.partial(kernel, count // 2, half),
        out_shape=(wide, wide, slim, slim),
        in_specs=[vmem] * 6,
        out_specs=(vmem,) * 4,
        scratch_shapes=[
            pltpu.VMEM(part, BF16),
            pltpu.VMEM(part, BF16),
            pltpu.VMEM((half, slots, rows, size), BF16),
            pltpu.VMEM((half, slots, rows, size), BF16),
            pltpu.VMEM((2, rows, WINDOW + rows), F32),
            pltpu.VMEM((2, slots, rows, size), F32),
            pltpu.VMEM(part, F32),
            pltpu.VMEM(part, BF16),
            pltpu.VMEM(part, BF16),
            pltpu.VMEM(part, BF16),
            pltpu.VMEM(part, BF16),
            pltpu.VMEM(part, BF16),
            pltpu.VMEM(part, BF16),
            pltpu.VMEM((half, 2, rows, size), BF16),
            dma((half, 4)), dma((half, 4)),
            dma((2, half, 2)), dma((2, half, 2)),
            dma((half, 2)), dma((half, 2)),
            dma((half,)), dma((half,)),
            dma((half,)), dma((half,)),
            dma((half, 2)), dma((half, 2)),
            dma((half, 2)), dma((half, 2)),
        ],
        compiler_params=pltpu.CompilerParams(
            collective_id=0, has_side_effects=True, vmem_limit_bytes=60 * 1024 * 1024
        ),
    )(
        paired(query_heads), paired(grad_out),
        jnp.transpose(key_heads, (1, 0, 2)), jnp.transpose(value_heads, (1, 0, 2)),
        q_docs, k_docs,
    )
    return (
        unpaired(attended), unpaired(grad_q),
        jnp.transpose(grad_k, (1, 0, 2)), jnp.transpose(grad_v, (1, 0, 2)),
    )


def solution(mesh):
    split = P(("dp", "ctx"), None, None)
    return jax.shard_map(
        body,
        mesh=mesh,
        in_specs=(split, split, split, split, P("dp")),
        out_specs=(split, split, split, split),
        check_vma=False,
    )
```

time: 365 us -> 112 us (0.31)
  the two profiles are of different devices: /device:TPU:8 before, /device:TPU:23 now
where the time goes in v1:
time: 112 us
  Pallas kernels  97.2 us (87%)
  local copies, waits for them, and re-layouts  14.1 us (13%)
    pallas_call x1, Pallas kernels, body(): pl.pallas_call(functools.partial(kernel, count // 2, half), out_shape=(wi...  97.2 us
    unnamed x20, local copies, waits for them, and re-layouts  11.4 us

profile of v1, /device:TPU:23, one launch (start us, length us, event | category | flops | bytes accessed | tf_op | source)
XLA Modules:
  0.0 112.0 jit_solution(4949312294501274443)
XLA Ops:
  0.6 0.0 copy-start.6
  0.7 0.7 copy-done.6
  1.3 0.1 dynamic_slice.6
  1.4 0.1 pad_dynamic-slice_fusion
  1.5 0.6 broadcast_in_dim.8.kd_ref
  2.1 0.9 copy.21.qd_ref
  2.9 0.0 copy-start
  3.0 2.6 %copy.17 = bf16[256,16,128]{2,0,1:T(8,128)(2,1)} copy(bf16[256,16,128]{2,1,0:T(8,128)(2,1)} %param.5) | data formatting | bytes 2097152 | tf_op args[0]
  5.5 0.0 copy-done
  5.5 0.0 copy-start.4
  5.5 0.0 copy-start.5
  5.5 1.2 %copy.18 = bf16[256,16,128]{2,0,1:T(8,128)(2,1)} copy(bf16[256,16,128]{2,1,0:T(8,128)(2,1)S(1)} %copy-done) | data formatting | bytes 2097152 | tf_op args[3]
  6.8 0.0 copy-done.4
  6.8 0.0 copy-done.5
  6.8 1.2 %copy_bitcast_fusion = (bf16[8,256,128]{2,1,0:T(8,128)(2,1)}, bf16[8,256,128]{2,1,0:T(8,128)(2,1)}) fusion(bf16[256,8,128]{2,1,0:T(8,128)(2,1)S(1)} %copy-done.4, bf16[256,8,128]{2,1,0:T(8,128)(2,1)S(1)} %copy-done.5), kind=kLoop, calls=%fused_computation | loop fusion | bytes 2097152 | tf_op jit(solution)/shard_map/transpose | solution.py:343
  7.9 97.2 %shard_map.84 = (bf16[8,2,256,128]{3,2,1,0:T(8,128)(2,1)}, bf16[8,2,256,128]{3,2,1,0:T(8,128)(2,1)}, bf16[8,256,128]{2,1,0:T(8,128)(2,1)}, bf16[8,256,128]{2,1,0:T(8,128)(2,1)}) custom-call(bf16[8,2,256,128]{3,2,1,0:T(8,128)(2,1)} %bitcast.19, bf16[8,2,256,128]{3,2,1,0:T(8,128)(2,1)} %bitcast.20, bf16[8,256,128]{2,1,0:T(8,128)(2,1)} %get-tuple-element.21.k_ref, ...), custom_call_target="tpu_custom_call" | custom-call | tf_op jit(solution)/shard_map/pallas_call | solution.py:310
  105.1 0.0 copy-start.1
  105.1 3.0 %copy.22 = bf16[256,16,128]{2,1,0:T(8,128)(2,1)} copy(bf16[256,16,128]{2,0,1:T(8,128)(2,1)} %bitcast.22) | data formatting | bytes 2097152
  108.1 0.0 copy-done.1
  108.1 1.6 %copy.23 = bf16[256,16,128]{2,1,0:T(8,128)(2,1)} copy(bf16[256,16,128]{2,0,1:T(8,128)(2,1)S(1)} %bitcast.21) | data formatting | bytes 2097152
  109.7 0.0 copy-done.3
  109.7 1.1 %copy.24 = bf16[256,8,128]{2,1,0:T(8,128)(2,1)} copy(bf16[256,8,128]{2,0,1:T(8,128)(2,1)S(1)} %bitcast.24) | data formatting | bytes 1048576
  110.9 0.0 copy-done.2
  110.9 1.1 %copy.25 = bf16[256,8,128]{2,1,0:T(8,128)(2,1)} copy(bf16[256,8,128]{2,0,1:T(8,128)(2,1)S(1)} %bitcast.23) | data formatting | bytes 1048576
  (2 shorter events, 0.0 us)
Async XLA Ops:
  0.6 0.7 copy-start.6
  2.9 2.6 %copy-start = (bf16[256,16,128]{2,1,0:T(8,128)(2,1)S(1)}, bf16[256,16,128]{2,1,0:T(8,128)(2,1)}, u32[]{:S(2)}) copy-start(bf16[256,16,128]{2,1,0:T(8,128)(2,1)} %param.8) | copy-start | bytes 3145732
  5.5 1.2 %copy-start.4 = (bf16[256,8,128]{2,1,0:T(8,128)(2,1)S(1)}, bf16[256,8,128]{2,1,0:T(8,128)(2,1)}, u32[]{:S(2)}) copy-start(bf16[256,8,128]{2,1,0:T(8,128)(2,1)} %param.7) | copy-start | bytes 1572868
  5.5 1.2 %copy-start.5 = (bf16[256,8,128]{2,1,0:T(8,128)(2,1)S(1)}, bf16[256,8,128]{2,1,0:T(8,128)(2,1)}, u32[]{:S(2)}) copy-start(bf16[256,8,128]{2,1,0:T(8,128)(2,1)} %param.6) | copy-start | bytes 1572868
  105.1 3.0 %copy-start.1 = (bf16[8,2,256,128]{3,2,1,0:T(8,128)(2,1)S(1)}, bf16[8,2,256,128]{3,2,1,0:T(8,128)(2,1)}, u32[]{:S(2)}) copy-start(bf16[8,2,256,128]{3,2,1,0:T(8,128)(2,1)} %get-tuple-element.9) | copy-start | bytes 3145732
  108.1 1.7 %copy-start.3 = (bf16[8,256,128]{2,1,0:T(8,128)(2,1)S(1)}, bf16[8,256,128]{2,1,0:T(8,128)(2,1)}, u32[]{:S(2)}) copy-start(bf16[8,256,128]{2,1,0:T(8,128)(2,1)} %get-tuple-element.10) | copy-start | bytes 1572868
  109.7 1.1 %copy-start.2 = (bf16[8,256,128]{2,1,0:T(8,128)(2,1)S(1)}, bf16[8,256,128]{2,1,0:T(8,128)(2,1)}, u32[]{:S(2)}) copy-start(bf16[8,256,128]{2,1,0:T(8,128)(2,1)} %get-tuple-element.11) | copy-start | bytes 1572868

commit v2 on v1

--- a/solution.py
+++ b/solution.py
@@ -118,17 +118,32 @@
 
         lax.fori_loop(0, half, step, 0)
 
-    def begin(hl):
+    def start_near(hl):
         @pl.when(has_next)
         def _():
             for to in range(2):
                 for copy in near_copies(hl, to):
                     copy.start()
 
+    def start_fwd(hl):
+        @pl.when(has_prev)
+        def _():
+            for sender in range(2):
+                for copy in near_arrivals(hl, sender):
+                    copy.wait_recv()
+
+        @pl.when(has_prev & has_next)
+        def _():
+            for copy in fwd_copies(hl):
+                copy.start()
+
+    start_near(0)
+
+    def start_swap(hl):
         for copy in swap_copies(hl):
             copy.start()
 
-    heads(begin)
+    heads(start_swap)
 
     def local(hl):
         kw[hl, 4 + c] = k_ref[mine + hl]
@@ -196,17 +211,6 @@
             mid_copy(hl).start()
 
     def stage(hl):
-        @pl.when(has_prev)
-        def _():
-            for sender in range(2):
-                for copy in near_arrivals(hl, sender):
-                    copy.wait_recv()
-
-        @pl.when(has_prev & has_next)
-        def _():
-            for copy in fwd_copies(hl):
-                copy.start()
-
         for copy in swap_copies(hl):
             copy.wait_recv()
 
@@ -215,10 +219,19 @@
             for copy in fwd_copies(hl):
                 copy.wait_recv()
 
+        @pl.when(hl + 1 < half)
+        def _():
+            start_near(hl + 1)
+
         acc[...] = jnp.zeros_like(acc)
 
         def per_piece(piece, carry):
             attend(hl, piece)
+
+            @pl.when((hl + 1 < half) & (piece == 0))
+            def _():
+                start_fwd(hl + 1)
+
             return carry
 
         lax.fori_loop(0, 2, per_piece, 0)
@@ -239,6 +252,7 @@
         def _():
             pass_mid(hl - 1)
 
+    start_fwd(0)
     heads(stage)
     pass_mid(half - 1)
 

time: 112 us -> 97.4 us (0.87)
  the two profiles are of different devices: /device:TPU:23 before, /device:TPU:8 now
where the time goes in v2:
time: 97.4 us; the launch traced here: 96.2 us
  Pallas kernels  81.4 us (84%)
  local copies, waits for them, and re-layouts  14.1 us (14%)
    pallas_call x1, Pallas kernels, body(): pl.pallas_call(functools.partial(kernel, count // 2, half), out_shape=(wi...  81.4 us
    unnamed x20, local copies, waits for them, and re-layouts  11.4 us

profile of v2, /device:TPU:8, one launch (start us, length us, event | category | flops | bytes accessed | tf_op | source)
XLA Modules:
  0.0 96.2 jit_solution(4017396505528976338)
XLA Ops:
  0.6 0.0 copy-start.6
  0.7 0.7 copy-done.6
  1.3 0.1 dynamic_slice.6
  1.4 0.1 pad_dynamic-slice_fusion
  1.5 0.6 broadcast_in_dim.8.kd_ref
  2.1 0.9 copy.21.qd_ref
  2.9 0.0 copy-start
  3.0 2.6 %copy.17 = bf16[256,16,128]{2,0,1:T(8,128)(2,1)} copy(bf16[256,16,128]{2,1,0:T(8,128)(2,1)} %param.5) | data formatting | bytes 2097152 | tf_op args[0]
  5.5 0.0 copy-done
  5.5 0.0 copy-start.4
  5.5 0.0 copy-start.5
  5.5 1.2 %copy.18 = bf16[256,16,128]{2,0,1:T(8,128)(2,1)} copy(bf16[256,16,128]{2,1,0:T(8,128)(2,1)S(1)} %copy-done) | data formatting | bytes 2097152 | tf_op args[3]
  6.8 0.0 copy-done.4
  6.8 0.0 copy-done.5
  6.8 1.2 %copy_bitcast_fusion = (bf16[8,256,128]{2,1,0:T(8,128)(2,1)}, bf16[8,256,128]{2,1,0:T(8,128)(2,1)}) fusion(bf16[256,8,128]{2,1,0:T(8,128)(2,1)S(1)} %copy-done.4, bf16[256,8,128]{2,1,0:T(8,128)(2,1)S(1)} %copy-done.5), kind=kLoop, calls=%fused_computation | loop fusion | bytes 2097152 | tf_op jit(solution)/shard_map/transpose | solution.py:357
  7.9 81.4 %shard_map.84 = (bf16[8,2,256,128]{3,2,1,0:T(8,128)(2,1)}, bf16[8,2,256,128]{3,2,1,0:T(8,128)(2,1)}, bf16[8,256,128]{2,1,0:T(8,128)(2,1)}, bf16[8,256,128]{2,1,0:T(8,128)(2,1)}) custom-call(bf16[8,2,256,128]{3,2,1,0:T(8,128)(2,1)} %bitcast.19, bf16[8,2,256,128]{3,2,1,0:T(8,128)(2,1)} %bitcast.20, bf16[8,256,128]{2,1,0:T(8,128)(2,1)} %get-tuple-element.21.k_ref, ...), custom_call_target="tpu_custom_call" | custom-call | tf_op jit(solution)/shard_map/pallas_call | solution.py:324
  89.3 0.0 copy-start.1
  89.3 3.0 %copy.22 = bf16[256,16,128]{2,1,0:T(8,128)(2,1)} copy(bf16[256,16,128]{2,0,1:T(8,128)(2,1)} %bitcast.22) | data formatting | bytes 2097152
  92.3 0.0 copy-done.1
  92.3 1.6 %copy.23 = bf16[256,16,128]{2,1,0:T(8,128)(2,1)} copy(bf16[256,16,128]{2,0,1:T(8,128)(2,1)S(1)} %bitcast.21) | data formatting | bytes 2097152
  93.9 0.0 copy-done.3
  93.9 1.1 %copy.24 = bf16[256,8,128]{2,1,0:T(8,128)(2,1)} copy(bf16[256,8,128]{2,0,1:T(8,128)(2,1)S(1)} %bitcast.24) | data formatting | bytes 1048576
  95.1 0.0 copy-done.2
  95.1 1.1 %copy.25 = bf16[256,8,128]{2,1,0:T(8,128)(2,1)} copy(bf16[256,8,128]{2,0,1:T(8,128)(2,1)S(1)} %bitcast.23) | data formatting | bytes 1048576
  (2 shorter events, 0.0 us)
Async XLA Ops:
  0.6 0.7 copy-start.6
  2.9 2.6 %copy-start = (bf16[256,16,128]{2,1,0:T(8,128)(2,1)S(1)}, bf16[256,16,128]{2,1,0:T(8,128)(2,1)}, u32[]{:S(2)}) copy-start(bf16[256,16,128]{2,1,0:T(8,128)(2,1)} %param.8) | copy-start | bytes 3145732
  5.5 1.2 %copy-start.4 = (bf16[256,8,128]{2,1,0:T(8,128)(2,1)S(1)}, bf16[256,8,128]{2,1,0:T(8,128)(2,1)}, u32[]{:S(2)}) copy-start(bf16[256,8,128]{2,1,0:T(8,128)(2,1)} %param.7) | copy-start | bytes 1572868
  5.5 1.2 %copy-start.5 = (bf16[256,8,128]{2,1,0:T(8,128)(2,1)S(1)}, bf16[256,8,128]{2,1,0:T(8,128)(2,1)}, u32[]{:S(2)}) copy-start(bf16[256,8,128]{2,1,0:T(8,128)(2,1)} %param.6) | copy-start | bytes 1572868
  89.3 3.0 %copy-start.1 = (bf16[8,2,256,128]{3,2,1,0:T(8,128)(2,1)S(1)}, bf16[8,2,256,128]{3,2,1,0:T(8,128)(2,1)}, u32[]{:S(2)}) copy-start(bf16[8,2,256,128]{3,2,1,0:T(8,128)(2,1)} %get-tuple-element.9) | copy-start | bytes 3145732
  92.3 1.7 %copy-start.3 = (bf16[8,256,128]{2,1,0:T(8,128)(2,1)S(1)}, bf16[8,256,128]{2,1,0:T(8,128)(2,1)}, u32[]{:S(2)}) copy-start(bf16[8,256,128]{2,1,0:T(8,128)(2,1)} %get-tuple-element.10) | copy-start | bytes 1572868
  93.9 1.1 %copy-start.2 = (bf16[8,256,128]{2,1,0:T(8,128)(2,1)S(1)}, bf16[8,256,128]{2,1,0:T(8,128)(2,1)}, u32[]{:S(2)}) copy-start(bf16[8,256,128]{2,1,0:T(8,128)(2,1)} %get-tuple-element.11) | copy-start | bytes 1572868

commit v3 on v2

--- a/solution.py
+++ b/solution.py
@@ -27,9 +27,9 @@
 
 def kernel(
     chips, half,
-    q_ref, g_ref, k_ref, v_ref, qd_ref, kd_ref,
+    q_in, g_in, k_ref, v_ref, docs_ref,
     o_ref, dq_ref, dk_ref, dv_ref,
-    qs, gs, kw, vw, bias, acc, own_s, far_s, far_r, mid_s, mid_r, o_s, dq_s, fin_s,
+    tall, q_ref, g_ref, qs, gs, kw, vw, bias, acc, own_s, far_s, far_r, mid_s, mid_r, o_s, dq_s, fin_s,
     swap_send, swap_recv, near_send, near_recv, fwd_send, fwd_recv,
     far_send, far_recv, mid_send, mid_recv, out_send, out_recv, fin_send, fin_recv,
 ):
@@ -139,6 +139,11 @@
 
     start_near(0)
 
+    for whole, split in ((q_in, q_ref), (g_in, g_ref)):
+        tall[...] = whole[...].astype(F32)
+        for head in range(2 * split.shape[0]):
+            split[head // 2, head % 2] = tall[:, head, :].astype(BF16)
+
     def start_swap(hl):
         for copy in swap_copies(hl):
             copy.start()
@@ -168,7 +173,11 @@
         lower = piece * rows
         q_index = lax.broadcasted_iota(jnp.int32, (rows, width), 0)
         k_index = lax.broadcasted_iota(jnp.int32, (rows, width), 1)
-        same = qd_ref[lower : lower + rows, :] == kd_ref[:, lower : lower + width]
+        first = pl.multiple_of(z * (2 * rows) + lower, rows)
+        k_docs = docs_ref[:, pl.ds(first, width)].astype(F32)
+        q_docs = docs_ref[:, pl.ds(first + WINDOW, rows)].astype(F32)
+        q_docs = jnp.transpose(jnp.broadcast_to(q_docs, (rows, rows)))[:, :1]
+        same = q_docs == k_docs
         allowed = same & (k_index > q_index) & (k_index <= q_index + WINDOW)
         bias[piece] = jnp.where(allowed, 0.0, MASKED).astype(F32)
 
@@ -303,14 +312,7 @@
     rows, groups, size = key_heads.shape
     half = groups // 2
     count = lax.axis_size("ctx")
-    chip = lax.div(lax.axis_index("ctx"), 2)
-    first_row = chip * (2 * rows)
-    pad_docs = jnp.concatenate([jnp.full((WINDOW,), -1, jnp.int32), doc_ids], 0)
-    q_docs = lax.dynamic_slice_in_dim(doc_ids, first_row, 2 * rows, 0)[:, None]
-    k_docs = lax.dynamic_slice_in_dim(pad_docs, first_row, WINDOW + 2 * rows, 0)[None, :]
-
-    def paired(x):
-        return jnp.transpose(x.reshape(rows, groups, 2, size), (1, 2, 0, 3))
+    pad_docs = jnp.concatenate([jnp.full((WINDOW,), -1, jnp.int32), doc_ids], 0)[None, :]
 
     def unpaired(x):
         return jnp.transpose(x, (2, 0, 1, 3)).reshape(query_heads.shape)
@@ -324,9 +326,12 @@
     attended, grad_q, grad_k, grad_v = pl.pallas_call(
         functools.partial(kernel, count // 2, half),
         out_shape=(wide, wide, slim, slim),
-        in_specs=[vmem] * 6,
+        in_specs=[vmem] * 5,
         out_specs=(vmem,) * 4,
         scratch_shapes=[
+            pltpu.VMEM(query_heads.shape, F32),
+            pltpu.VMEM((groups, 2, rows, size), BF16),
+            pltpu.VMEM((groups, 2, rows, size), BF16),
             pltpu.VMEM(part, BF16),
             pltpu.VMEM(part, BF16),
             pltpu.VMEM((half, slots, rows, size), BF16),
@@ -353,9 +358,9 @@
             collective_id=0, has_side_effects=True, vmem_limit_bytes=60 * 1024 * 1024
         ),
     )(
-        paired(query_heads), paired(grad_out),
+        query_heads, grad_out,
         jnp.transpose(key_heads, (1, 0, 2)), jnp.transpose(value_heads, (1, 0, 2)),
-        q_docs, k_docs,
+        pad_docs,
     )
     return (
         unpaired(attended), unpaired(grad_q),

time: 97.4 us -> 94.3 us (0.968)
  local copies, waits for them, and re-layouts: 14.1 us -> 10.5 us
    unnamed x20 -> x10, local copies, waits for them, and re-layouts: 11.4 us -> 6.89 us
    broadcast_in_dim x2 -> x0, local copies, waits for them, and re-layouts: 1.46 us -> none  [the longest x1 0.86 us: body(): q_docs = lax.dynamic_slice_in_dim(doc_ids, first_row, 2 * rows, 0)[:, None]]
    concatenate x0 -> x1, local copies, waits for them, and re-layouts: none -> 1.3 us  [body(): jnp.concatenate([jnp.full((WINDOW,), -1, jnp.int32), doc_ids], 0)[None, :]]
    transpose x1, local copies, waits for them, and re-layouts: 1.15 us -> 2.35 us  [body(): jnp.transpose(value_heads, (1, 0, 2))]
where the time goes in v3:
time: 94.3 us; the launch traced here: 92.5 us
  Pallas kernels  81.3 us (86%)
  local copies, waits for them, and re-layouts  10.5 us (11%)
    pallas_call x1, Pallas kernels, body(): pl.pallas_call(functools.partial(kernel, count // 2, half), out_shape=(wi...  81.3 us
    unnamed x10, local copies, waits for them, and re-layouts  6.89 us
    transpose x1, local copies, waits for them, and re-layouts, body(): jnp.transpose(value_heads, (1, 0, 2))  2.35 us

profile of v3, /device:TPU:8, one launch (start us, length us, event | category | flops | bytes accessed | tf_op | source)
XLA Modules:
  0.0 92.5 jit_solution(11922224030787815064)
XLA Ops:
  0.6 1.3 %concatenate.3 = s32[3072]{0:T(1024)} pad(s32[2048]{0:T(1024)} %param.9, s32[]{:T(128)} %constant.0.clone.1), padding=1024_0 | pad | bytes 20484 | tf_op jit(solution)/shard_map/concatenate | solution.py:315
  1.9 2.4 %copy_bitcast_fusion = (bf16[8,256,128]{2,1,0:T(8,128)(2,1)}, bf16[8,256,128]{2,1,0:T(8,128)(2,1)}) fusion(bf16[256,8,128]{2,1,0:T(8,128)(2,1)} %param.7, bf16[256,8,128]{2,1,0:T(8,128)(2,1)} %param.6), kind=kLoop, calls=%fused_computation | loop fusion | bytes 2097152 | tf_op jit(solution)/shard_map/transpose | solution.py:362
  4.3 81.3 %shard_map.84 = (bf16[8,2,256,128]{3,2,1,0:T(8,128)(2,1)}, bf16[8,2,256,128]{3,2,1,0:T(8,128)(2,1)}, bf16[8,256,128]{2,1,0:T(8,128)(2,1)}, bf16[8,256,128]{2,1,0:T(8,128)(2,1)}) custom-call(bf16[256,16,128]{2,1,0:T(8,128)(2,1)} %q_in.1, bf16[256,16,128]{2,1,0:T(8,128)(2,1)} %g_in.1, bf16[8,256,128]{2,1,0:T(8,128)(2,1)} %get-tuple-element.17.k_ref, ...), custom_call_target="tpu_custom_call" | custom-call | tf_op jit(solution)/shard_map/pallas_call | solution.py:326
  85.6 0.0 copy-start
  85.6 3.0 %copy.11 = bf16[256,16,128]{2,1,0:T(8,128)(2,1)} copy(bf16[256,16,128]{2,0,1:T(8,128)(2,1)} %bitcast.14) | data formatting | bytes 2097152
  88.6 0.0 copy-done
  88.6 0.0 copy-start.2
  88.6 1.6 %copy.12 = bf16[256,16,128]{2,1,0:T(8,128)(2,1)} copy(bf16[256,16,128]{2,0,1:T(8,128)(2,1)S(1)} %bitcast.13) | data formatting | bytes 2097152
  90.2 0.0 copy-done.2
  90.2 0.0 copy-start.1
  90.2 1.1 %copy.13 = bf16[256,8,128]{2,1,0:T(8,128)(2,1)} copy(bf16[256,8,128]{2,0,1:T(8,128)(2,1)S(1)} %bitcast.16) | data formatting | bytes 1048576
  91.4 0.0 copy-done.1
  91.4 1.1 %copy.14 = bf16[256,8,128]{2,1,0:T(8,128)(2,1)} copy(bf16[256,8,128]{2,0,1:T(8,128)(2,1)S(1)} %bitcast.15) | data formatting | bytes 1048576
Async XLA Ops:
  85.6 3.0 %copy-start = (bf16[8,2,256,128]{3,2,1,0:T(8,128)(2,1)S(1)}, bf16[8,2,256,128]{3,2,1,0:T(8,128)(2,1)}, u32[]{:S(2)}) copy-start(bf16[8,2,256,128]{3,2,1,0:T(8,128)(2,1)} %get-tuple-element.9) | copy-start | bytes 3145732
  88.6 1.7 %copy-start.2 = (bf16[8,256,128]{2,1,0:T(8,128)(2,1)S(1)}, bf16[8,256,128]{2,1,0:T(8,128)(2,1)}, u32[]{:S(2)}) copy-start(bf16[8,256,128]{2,1,0:T(8,128)(2,1)} %get-tuple-element.10) | copy-start | bytes 1572868
  90.2 1.1 %copy-start.1 = (bf16[8,256,128]{2,1,0:T(8,128)(2,1)S(1)}, bf16[8,256,128]{2,1,0:T(8,128)(2,1)}, u32[]{:S(2)}) copy-start(bf16[8,256,128]{2,1,0:T(8,128)(2,1)} %get-tuple-element.11) | copy-start | bytes 1572868
